TPU v7x, 32 devices: a whole 2x2x4 slice. The times are simulated.
32 devices in a mesh: groups: 2 (over y), expert: 4 (over z), dp: 4 (over x, core).
Axes of the slice: x: 2, y: 2, z: 4, core: 2. Of those that a mesh axis runs over, the one named last changes fastest.
Arguments:
- tokens: bfloat16 [1024, 4096], P(('groups', 'expert'), 'dp'), parts along dimension 0, may hold values from -6 to 6
- routes: int32 [1024, 4], P(('groups', 'expert')), parts along dimension 0, may hold values from 0 to 7, all different within a row; in each aligned block of 128 rows (0 to 127, 128 to 255, ...) at most 128 rows name the same one
- gates: float32 [1024, 4], P(('groups', 'expert')), parts along dimension 0, may hold values from 0.05 to 1
- w_in: bfloat16 [4096, 1024], P(('dp', 'expert')), may hold values from -0.09375 to 0.09375
- w_out: bfloat16 [4096, 1024], P(('dp', 'expert')), may hold values from -0.1875 to 0.1875
- w_first: bfloat16 [8, 1024, 1024], P('expert', None, 'dp'), may hold values from -0.1875 to 0.1875
- w_second: bfloat16 [8, 1024, 1024], P('expert', 'dp'), may hold values from -0.1875 to 0.1875
- out_grad: bfloat16 [1024, 4096], P(('groups', 'expert'), 'dp'), parts along dimension 0, may hold values from -6 to 6
Outputs:
- mixed: bfloat16 [1024, 4096], P(('groups', 'expert'), 'dp'), parts along dimension 0
- grad_tokens: bfloat16 [1024, 4096], P(('groups', 'expert'), 'dp'), parts along dimension 0
- grad_w_in: float32 [8192, 1024], P(('groups', 'dp', 'expert')), parts along dimension 0
- grad_w_out: float32 [8192, 1024], P(('groups', 'dp', 'expert')), parts along dimension 0
- grad_first: bfloat16 [16, 1024, 1024], P(('groups', 'expert'), None, 'dp'), parts along dimension 0
- grad_second: bfloat16 [16, 1024, 1024], P(('groups', 'expert'), 'dp'), parts along dimension 0
There are 2 independent parts, one for each index of `groups`. A program takes and returns all parts, laid end to end along the dimension named above; an argument that names none is the same for every part. Nothing has to cross between parts.
Inputs may be any that keep to these rules, and one draw needn't show every extreme that they name: `routes`: each row names 4 different experts. Within each aligned block of 128 rows no expert is named by more than 128 rows, a bound that some block reaches.
All inputs are finite; a program needn't handle non-finite values.
Results may differ from a plain program's by a relative error of at most 0.025.
Values may be sent and summed in bfloat16 or wider, within the bound.
A program may use at most 64 MiB of HBM per device.

v0:
```python
import jax
import jax.numpy as jnp
from jax import lax
from jax.sharding import PartitionSpec as P


def body(tokens, routes, gates, w_in, w_out, w_first, w_second, out_grad):
    in_full, out_full = (
        lax.all_gather(w_in, "expert", axis=0, tiled=True),
        lax.all_gather(w_out, "expert", axis=0, tiled=True),
    )
    token_count = tokens.shape[0]
    top_count = routes.shape[1]
    expert_local = w_first.shape[0]
    expert_shards = lax.axis_size("expert")
    expert_total = expert_local * expert_shards
    latent_width = w_in.shape[1]
    capacity = min(token_count, max(2, 5 * token_count * top_count // (2 * expert_total)))
    flat = routes.reshape(-1)
    onehot = (flat[:, None] == jnp.arange(expert_total, dtype=jnp.int32)[None, :]).astype(jnp.int32)
    slot = jnp.sum(onehot * (jnp.cumsum(onehot, axis=0) - 1), axis=1)
    dest = flat * capacity + slot
    weights = gates.reshape(-1, 1)

    def dp_total(value):
        return lax.psum(value.astype(jnp.bfloat16), "dp").astype(jnp.float32)

    def pack(route_rows):
        buffer = (
            jnp.zeros((expert_total * capacity, route_rows.shape[1]), route_rows.dtype)
            .at[dest]
            .set(route_rows)
        )
        return buffer.reshape(expert_shards, expert_local, capacity, route_rows.shape[1])

    def send(route_rows):
        share = latent_width // lax.axis_size("dp")
        columns = lax.dynamic_slice_in_dim(route_rows, lax.axis_index("dp") * share, share, 1)
        moved = lax.all_to_all(pack(columns), "expert", split_axis=0, concat_axis=0, tiled=True)
        return lax.all_gather(moved, "dp", axis=3, tiled=True)

    def combine_rows(buffer, scale):
        returned = lax.all_to_all(buffer, "expert", split_axis=0, concat_axis=0, tiled=True)
        rows = returned.reshape(expert_total * capacity, latent_width)[dest].astype(jnp.float32)
        if scale is not None:
            rows = scale * rows
        summed = jnp.sum(rows.reshape(token_count, top_count, latent_width), axis=1)
        return dp_total(summed).astype(jnp.bfloat16)

    latent = dp_total(jnp.dot(tokens, in_full, preferred_element_type=jnp.float32)).astype(
        jnp.bfloat16
    )
    arrived = send(jnp.repeat(latent, top_count, axis=0))
    before = jnp.einsum("sjcl,jlh->sjch", arrived, w_first, preferred_element_type=jnp.float32)
    hidden = jnp.square(jax.nn.relu(before)).astype(jnp.bfloat16)
    partial_out = jnp.einsum(
        "sjch,jhl->sjcl", hidden, w_second, preferred_element_type=jnp.float32
    ).astype(jnp.bfloat16)
    lat_out = combine_rows(partial_out, weights)
    mixed = jnp.dot(lat_out, out_full.T, preferred_element_type=jnp.float32).astype(jnp.bfloat16)
    grad_latent = dp_total(jnp.dot(out_grad, out_full, preferred_element_type=jnp.float32)).astype(
        jnp.bfloat16
    )
    route_grad = (weights * jnp.repeat(grad_latent, top_count, axis=0).astype(jnp.float32)).astype(
        jnp.bfloat16
    )
    incoming = send(route_grad)
    hidden_grad = jnp.einsum(
        "sjcl,jhl->sjch", incoming, w_second, preferred_element_type=jnp.float32
    )
    before_grad = (hidden_grad * 2.0 * jax.nn.relu(before)).astype(jnp.bfloat16)
    grad_second = jnp.einsum(
        "sjch,sjcl->jhl", hidden, incoming, preferred_element_type=jnp.float32
    ).astype(jnp.bfloat16)
    grad_first = jnp.einsum(
        "sjcl,sjch->jlh", arrived, before_grad, preferred_element_type=jnp.float32
    ).astype(jnp.bfloat16)
    back_piece = jnp.einsum(
        "sjch,jlh->sjcl", before_grad, w_first, preferred_element_type=jnp.float32
    ).astype(jnp.bfloat16)
    grad_in = combine_rows(back_piece, None)
    grad_tokens = jnp.dot(grad_in, in_full.T, preferred_element_type=jnp.float32).astype(
        jnp.bfloat16
    )
    first_term = jnp.dot(tokens.T, grad_in, preferred_element_type=jnp.float32)
    second_term = jnp.dot(out_grad.T, lat_out, preferred_element_type=jnp.float32)
    sums = lax.psum_scatter(
        jnp.concatenate([first_term, second_term], axis=1).astype(jnp.bfloat16),
        "expert",
        scatter_dimension=0,
        tiled=True,
    ).astype(jnp.float32)
    return (
        mixed,
        grad_tokens,
        sums[:, :latent_width],
        sums[:, latent_width:],
        grad_first,
        grad_second,
    )


def solution(mesh):
    placed = (
        P(("groups", "expert"), "dp"),
        P(("groups", "expert"), None),
        P(("groups", "expert"), None),
        P(("dp", "expert"), None),
        P(("dp", "expert"), None),
        P("expert", None, "dp"),
        P("expert", "dp", None),
        P(("groups", "expert"), "dp"),
    )
    return jax.shard_map(
        body,
        mesh=mesh,
        in_specs=placed,
        out_specs=(
            P(("groups", "expert"), "dp"),
            P(("groups", "expert"), "dp"),
            P(("groups", "dp", "expert"), None),
            P(("groups", "dp", "expert"), None),
            P(("groups", "expert"), None, "dp"),
            P(("groups", "expert"), "dp", None),
        ),
        check_vma=False,
    )
```

profile of v0, /device:TPU:0, one launch (start us, length us, event | category | flops | bytes accessed | tf_op | source)
XLA Modules:
  0.0 426.0 jit_solution(858944117006352441)
XLA Ops:
  8.0 0.7 all-gather.5.cloned.1.call-update
  8.7 0.8 copy.34
  9.7 1.1 reduce-window.6
  11.2 0.7 broadcast_multiply_fusion
  11.8 46.4 %all-gather.9.cloned.1.call-done = bf16[1024,1024]{1,0:T(8,128)(2,1)} async-done(((bf16[256,1024]{1,0:T(8,128)(2,1)}), bf16[1024,1024]{1,0:T(8,128)(2,1)}) %all-gather.9.cloned.1.call-update) | async-done | bytes 2097168 | tf_op jit(solution)/shard_map/all_gather | solution.py:10
  58.3 2.8 convolution_convert_fusion.1
  61.1 43.4 %all-gather.5.cloned.1.call-done = bf16[1024,1024]{1,0:T(8,128)(2,1)} async-done(((bf16[256,1024]{1,0:T(8,128)(2,1)}), bf16[1024,1024]{1,0:T(8,128)(2,1)}) %all-gather.5.cloned.1.call-update) | async-done | bytes 2097168 | tf_op jit(solution)/shard_map/all_gather | solution.py:9
  104.5 2.7 convolution_convert_fusion.3
  107.7 31.8 %all-reduce.7.cloned.1.call-done = (bf16[128,1024]{1,0:T(8,128)(2,1)}, bf16[128,1024]{1,0:T(8,128)(2,1)}) async-done(((bf16[128,1024]{1,0:T(8,128)(2,1)}, bf16[128,1024]{1,0:T(8,128)(2,1)}), (bf16[128,1024]{1,0:T(8,128)(2,1)}, bf16[128,1024]{1,0:T(8,128)(2,1)})) %all-reduce.7.cloned.1.call-update) | async-done | bytes 524304 | tf_op jit(solution)/shard_map/psum | solution.py:26
  139.5 1.3 broadcast_in_dim.4
  141.1 2.5 scatter_custom_fusion
  143.6 18.0 %all_to_all.20 = bf16[4,2,128,256]{3,2,1,0:T(8,128)(2,1)S(1)} all-to-all(bf16[4,2,128,256]{3,2,1,0:T(8,128)(2,1)S(1)} %bitcast.68), channel_id=1, replica_groups=mesh['groups'=2,'expert'=4,'dp'=4] {'expert'}, dimensions={0} | all-to-all | bytes 1048576 | tf_op jit(solution)/shard_map/all_to_all | solution.py:39
  161.5 0.8 copy.36
  163.2 1.8 convert_element_type.94
  165.0 3.1 scatter_custom_fusion.1
  168.1 16.3 %all_to_all.21 = bf16[4,2,128,256]{3,2,1,0:T(8,128)(2,1)S(1)} all-to-all(bf16[4,2,128,256]{3,2,1,0:T(8,128)(2,1)S(1)} %bitcast.67), channel_id=1, replica_groups=mesh['groups'=2,'expert'=4,'dp'=4] {'expert'}, dimensions={0} | all-to-all | bytes 1048576 | tf_op jit(solution)/shard_map/all_to_all | solution.py:39
  184.5 0.8 copy.39
  185.3 2.3 convolution_maximum_fusion
  187.7 1.0 copy-done.1
  188.6 0.7 convert_bitcast_fusion.3
  189.4 1.5 copy.37
  190.9 3.7 all-to-all-start.1
  194.6 13.8 %all-gather.11.cloned.1.call-done = bf16[4,2,128,1024]{3,2,0,1:T(8,128)(2,1)} async-done(((bf16[4,2,128,256]{3,2,0,1:T(8,128)(2,1)}), bf16[4,2,128,1024]{3,2,0,1:T(8,128)(2,1)}) %all-gather.11.cloned.1.call-update) | async-done | bytes 2097168 | tf_op jit(solution)/shard_map/all_gather | solution.py:40
  208.4 2.7 fusion.2
  211.1 0.8 copy-done.7
  211.9 0.7 convert_bitcast_fusion.2
  212.6 1.5 copy.40
  214.1 28.1 %all-to-all-done.1 = bf16[4,2,128,1024]{3,2,1,0:T(8,128)(2,1)S(1)} async-done(((bf16[4,2,128,1024]{3,2,1,0:T(8,128)(2,1)}), bf16[4,2,128,1024]{3,2,1,0:T(8,128)(2,1)S(1)}, u32[]{:S(2)}, u32[]{:S(2)}) %all-to-all-start.1) | async-done | bytes 2097184 | tf_op jit(solution)/shard_map/all_to_all | solution.py:43
  242.3 4.5 %all-to-all-start.3 = ((bf16[4,2,128,1024]{3,2,1,0:T(8,128)(2,1)}), bf16[4,2,128,1024]{3,2,1,0:T(8,128)(2,1)}, u32[]{:S(2)}, u32[]{:S(2)}) async-start(bf16[4,2,128,1024]{3,2,1,0:T(8,128)(2,1)} %copy.40), calls=%async_computation.3 | async-start | bytes 4194304 | tf_op jit(solution)/shard_map/all_to_all | solution.py:43
  247.0 2.8 gather_fusion
  249.8 1.7 reshape.96
  251.5 2.1 multiply_reduce_fusion
  253.6 40.9 %all-to-all-done.3 = bf16[4,2,128,1024]{3,2,1,0:T(8,128)(2,1)} async-done(((bf16[4,2,128,1024]{3,2,1,0:T(8,128)(2,1)}), bf16[4,2,128,1024]{3,2,1,0:T(8,128)(2,1)}, u32[]{:S(2)}, u32[]{:S(2)}) %all-to-all-start.3) | async-done | bytes 2097184 | tf_op jit(solution)/shard_map/all_to_all | solution.py:43
  294.5 4.6 %gather_fusion.1 = bf16[512,1024]{1,0:T(8,128)(2,1)S(1)} fusion(bf16[1024,1024]{1,0:T(8,128)(2,1)} %bitcast.17, s32[1024]{0:T(1024)S(1)} %pad_clamp_fusion), kind=kCustom, calls=%fused_computation.1 | custom fusion | bytes 2099200 | tf_op jit(solution)/shard_map/gather | solution.py:44
  299.5 2.1 reduce_sum.35
  301.7 31.4 %all-reduce.5.cloned.1.call-done = (bf16[128,1024]{1,0:T(8,128)(2,1)}, bf16[128,1024]{1,0:T(8,128)(2,1)}) async-done(((bf16[128,1024]{1,0:T(8,128)(2,1)}, bf16[128,1024]{1,0:T(8,128)(2,1)}), (bf16[128,1024]{1,0:T(8,128)(2,1)}, bf16[128,1024]{1,0:T(8,128)(2,1)})) %all-reduce.5.cloned.1.call-update) | async-done | bytes 524304 | tf_op jit(solution)/shard_map/psum | solution.py:26
  333.2 1.7 convert_bitcast_fusion
  334.9 0.7 convert_bitcast_fusion.1
  335.6 2.4 pad_maximum_fusion
  338.1 1.6 copy-done.5
  339.6 3.1 bitcast_convert_fusion.1
  342.7 1.7 bitcast_convert_fusion
  344.5 1.5 convolution_convert_fusion
  346.4 1.5 convolution_convert_fusion.2
  347.9 67.2 %reduce-scatter.2.cloned.1.call-done = bf16[256,2048]{0,1:T(8,128)(2,1)} async-done(((bf16[1024,2048]{0,1:T(8,128)(2,1)}), bf16[256,2048]{0,1:T(8,128)(2,1)}) %reduce-scatter.2.cloned.1.call-update) | async-done | bytes 1048592 | tf_op jit(solution)/shard_map/reduce_scatter | solution.py:87
  415.2 1.4 fusion.20
  416.5 1.3 copy.44
  417.8 1.3 copy.43
  (63 shorter events, 3.9 us)
Async XLA Ops:
  7.2 181.5 %copy-start = (bf16[2,256,1024]{2,1,0:T(8,128)(2,1)S(1)}, bf16[2,256,1024]{2,1,0:T(8,128)(2,1)}, u32[]{:S(2)}) copy-start(bf16[2,256,1024]{2,1,0:T(8,128)(2,1)} %param.14) | copy-start | bytes 3145732
  7.2 97.4 %copy-start.11 = (bf16[128,1024]{1,0:T(8,128)(2,1)S(1)}, bf16[128,1024]{1,0:T(8,128)(2,1)}, u32[]{:S(2)}) copy-start(bf16[128,1024]{1,0:T(8,128)(2,1)} %param.8) | copy-start | bytes 786436
  7.2 51.1 %all-gather.9.cloned.1.call-start = ((), (), s32[]{:S(2)}) async-start(), calls=%async_computation.7 | async-start | bytes 2621440 | tf_op jit(solution)/shard_map/all_gather | solution.py:10
  7.9 96.6 %all-gather.5.cloned.1.call-start = ((), (), s32[]{:S(2)}) async-start(), calls=%async_computation.5 | async-start | bytes 2621440 | tf_op jit(solution)/shard_map/all_gather | solution.py:9
  8.7 130.8 %all-reduce.7.cloned.1.call-start = ((), (), s32[]{:S(2)}) async-start(), calls=%async_computation.11 | async-start | bytes 1048576 | tf_op jit(solution)/shard_map/psum | solution.py:26
  107.3 78.0 %all-gather.7.cloned.1.call-start = ((), (), s32[]{:S(2)}) async-start(), calls=%async_computation.6 | async-start | bytes 2621440 | tf_op jit(solution)/shard_map/all_gather | solution.py:40
  141.0 21.4 %copy-start.17 = (f32[128,4]{0,1:T(4,128)S(1)}, f32[128,4]{0,1:T(4,128)}, u32[]{:S(2)}) copy-start(f32[128,4]{0,1:T(4,128)} %param.10) | copy-start | bytes 6148
  141.0 21.6 %copy-start.16 = (bf16[128,1024]{1,0:T(8,128)(2,1)S(1)}, bf16[128,1024]{1,0:T(8,128)(2,1)}, u32[]{:S(2)}) copy-start(bf16[128,1024]{1,0:T(8,128)(2,1)} %get-tuple-element.26) | copy-start | bytes 786436
  162.4 46.0 %all-gather.11.cloned.1.call-start = ((), (), s32[]{:S(2)}) async-start(), calls=%async_computation.8 | async-start | bytes 2621440 | tf_op jit(solution)/shard_map/all_gather | solution.py:40
  165.0 20.4 %copy-start.8 = (bf16[2,1024,256]{2,1,0:T(8,128)(2,1)S(1)}, bf16[2,1024,256]{2,1,0:T(8,128)(2,1)}, u32[]{:S(2)}) copy-start(bf16[2,1024,256]{2,1,0:T(8,128)(2,1)} %param.13) | copy-start | bytes 3145732
  187.7 1.0 copy-start.1
  190.9 51.4 %all-to-all-start.1 = ((bf16[4,2,128,1024]{3,2,1,0:T(8,128)(2,1)}), bf16[4,2,128,1024]{3,2,1,0:T(8,128)(2,1)S(1)}, u32[]{:S(2)}, u32[]{:S(2)}) async-start(bf16[4,2,128,1024]{3,2,1,0:T(8,128)(2,1)} %copy.37), calls=%async_computation.1 | async-start | bytes 4194304 | tf_op jit(solution)/shard_map/all_to_all | solution.py:43
  208.4 3.5 copy-start.9
  211.1 0.8 copy-start.7
  242.3 52.2 %all-to-all-start.3 = ((bf16[4,2,128,1024]{3,2,1,0:T(8,128)(2,1)}), bf16[4,2,128,1024]{3,2,1,0:T(8,128)(2,1)}, u32[]{:S(2)}, u32[]{:S(2)}) async-start(bf16[4,2,128,1024]{3,2,1,0:T(8,128)(2,1)} %copy.40), calls=%async_computation.3 | async-start | bytes 4194304 | tf_op jit(solution)/shard_map/all_to_all | solution.py:43
  246.7 86.4 %all-reduce.5.cloned.1.call-start = ((), (), s32[]{:S(2)}) async-start(), calls=%async_computation.10 | async-start | bytes 1048576 | tf_op jit(solution)/shard_map/psum | solution.py:26
  299.1 34.1 %copy-start.10 = (bf16[128,1024]{1,0:T(8,128)(2,1)S(1)}, bf16[128,1024]{1,0:T(8,128)(2,1)}, u32[]{:S(2)}) copy-start(bf16[128,1024]{1,0:T(8,128)(2,1)} %param.15) | copy-start | bytes 786436
  299.5 35.4 %copy-start.12 = (bf16[128,1024]{1,0:T(8,128)(2,1)S(1)}, bf16[128,1024]{1,0:T(8,128)(2,1)}, u32[]{:S(2)}) copy-start(bf16[128,1024]{1,0:T(8,128)(2,1)} %param.8) | copy-start | bytes 786436
  301.7 113.5 %reduce-scatter.2.cloned.1.call-start = ((), (), s32[]{:S(2)}) async-start(), calls=%async_computation.9 | async-start | bytes 5242880 | tf_op jit(solution)/shard_map/reduce_scatter | solution.py:87
  333.2 1.7 copy-start.14
  338.0 1.6 copy-start.5
  339.6 3.1 copy-start.2
  339.6 3.1 copy-start.6
  342.7 1.7 copy-start.4
  342.7 1.7 copy-start.15
  344.5 1.8 copy-start.3
  344.5 1.9 copy-start.13
Sparse Core Ops, SparseCore 0:
  9.6 48.6 all-gather.8
  59.8 44.6 all-gather.4
  107.5 31.8 all-reduce.6
  162.5 20.9 all-gather.6
  185.5 22.8 all-gather.10
  301.8 31.3 all-reduce.4
  338.2 76.9 reduce-scatter.1
where the time goes:
time: 427 us; the launch traced here: 426 us
  waiting for transfers between devices  305 us (71%)
  blocking collectives  34.3 us (8%)
  local copies, waits for them, and re-layouts  29.9 us (7%)
  matrix products  22.4 us (5%)
  between operations  14.4 us (3%)
  other arithmetic  11.7 us (3%)
  starting transfers between devices  8.68 us (2%)
    all_to_all x2, waiting for transfers between devices, combine_rows(): lax.all_to_all(buffer, 'expert', split_axis=0, concat_axis=0, tiled=True)  69.1 us
    reduce_scatter x1, waiting for transfers between devices, body(): lax.psum_scatter(jnp.concatenate([first_term, second_term], axis=1).astyp...  67.2 us
    psum x2, waiting for transfers between devices, dp_total(): return lax.psum(value.astype(jnp.bfloat16), 'dp').astype(jnp.float32)  63.2 us
    all_gather x1, waiting for transfers between devices, body(): lax.all_gather(w_out, 'expert', axis=0, tiled=True)  46.4 us
    all_gather x1, waiting for transfers between devices, body(): lax.all_gather(w_in, 'expert', axis=0, tiled=True)  43.4 us
    all_to_all x2, blocking collectives, send(): lax.all_to_all(pack(columns), 'expert', split_axis=0, concat_axis=0, tile...  34.3 us
    all_gather x2, waiting for transfers between devices, send(): return lax.all_gather(moved, 'dp', axis=3, tiled=True)  13.8 us
  transfers between devices with their start and end apart: 9, of which 8 were waited for; matrix products, arithmetic and copies ran while one was open for 9% of the time, Pallas kernels for 0%

commit v1 on v0

--- a/solution.py
+++ b/solution.py
@@ -100,6 +100,67 @@
     )
 
 
+def dense_body(tokens, routes, gates, w_in, w_out, w_first, w_second, out_grad):
+    bf16, f32 = jnp.bfloat16, jnp.float32
+    shards = lax.axis_size("expert")
+    local, latent_width, hidden_width = w_first.shape
+    depth = w_in.shape[0]
+
+    def dot(a, b, dims):
+        return lax.dot_general(a, b, (dims, ((), ())), preferred_element_type=f32)
+
+    def total(value):
+        return lax.psum(value.astype(bf16), ("expert", "dp"))
+
+    def to_columns(value):
+        return lax.all_to_all(value, "expert", split_axis=1, concat_axis=0, tiled=True)
+
+    def to_rows(value):
+        return lax.all_to_all(value, "expert", split_axis=0, concat_axis=1, tiled=True)
+
+    experts = lax.axis_index("expert") * local + jnp.arange(local, dtype=jnp.int32)
+    named = lax.all_gather(
+        jnp.sum(
+            jnp.where(
+                routes[:, :, None] == jnp.arange(local * shards, dtype=jnp.int32), gates[:, :, None], 0.0
+            ),
+            axis=1,
+        ),
+        "expert",
+        axis=0,
+        tiled=True,
+    )
+    share = jnp.repeat(jnp.take(named, experts, axis=1), hidden_width, axis=1)
+    tok, grad = to_columns(tokens), to_columns(out_grad)
+    first = jnp.swapaxes(w_first, 0, 1).reshape(latent_width, local * hidden_width)
+    second = w_second.reshape(local * hidden_width, latent_width)
+    latent = total(dot(tok, w_in, ((1,), (0,))))
+    grad_latent = total(dot(grad, w_out, ((1,), (0,))))
+    active = jnp.maximum(dot(latent, first, ((1,), (0,))), 0.0)
+    hidden = (share * active * active).astype(bf16)
+    lat_out = total(dot(hidden, second, ((1,), (0,))))
+    slope = (dot(grad_latent, second, ((1,), (1,))) * share * (2.0 * active)).astype(bf16)
+    grad_in = total(dot(slope, first, ((1,), (1,))))
+    grad_second = dot(hidden, grad_latent, ((0,), (0,))).astype(bf16)
+    grad_first = dot(latent, slope, ((0,), (0,))).astype(bf16)
+    return (
+        to_rows(dot(lat_out, w_out, ((1,), (1,))).astype(bf16)),
+        to_rows(dot(grad_in, w_in, ((1,), (1,))).astype(bf16)),
+        dot(tok, grad_in, ((0,), (0,))),
+        dot(grad, lat_out, ((0,), (0,))),
+        jnp.swapaxes(grad_first.reshape(latent_width, local, hidden_width), 0, 1),
+        grad_second.reshape(local, hidden_width, latent_width),
+    )
+
+
+def layer(*args):
+    tokens, routes, w_first = args[0], args[1], args[5]
+    count, experts = tokens.shape[0], w_first.shape[0] * lax.axis_size("expert")
+    if 5 * count * routes.shape[1] // (2 * experts) >= count:
+        return dense_body(*args)
+    return body(*args)
+
+
 def solution(mesh):
     placed = (
         P(("groups", "expert"), "dp"),
@@ -112,7 +173,7 @@
         P(("groups", "expert"), "dp"),
     )
     return jax.shard_map(
-        body,
+        layer,
         mesh=mesh,
         in_specs=placed,
         out_specs=(

time: 427 us -> 272 us (0.64)
  waiting for transfers between devices: 305 us -> 193 us
  blocking collectives: 34.3 us -> 13.1 us
  local copies, waits for them, and re-layouts: 29.9 us -> 14.4 us
  other arithmetic: 11.7 us -> 0.1 us
  starting transfers between devices: 8.68 us -> 17 us
    psum x2, waiting for transfers between devices: 63.2 us -> 175 us  [total(): return lax.psum(value.astype(bf16), ('expert', 'dp'))]
    all_gather x4 -> x0, waiting for transfers between devices: 104 us -> none  [the longest x1 46.4 us: body(): lax.all_gather(w_out, 'expert', axis=0, tiled=True)]
    reduce_scatter x1 -> x0, waiting for transfers between devices: 67.2 us -> none  [body(): lax.psum_scatter(jnp.concatenate([first_term, second_term], axis=1).astyp...]
    all_to_all x2 -> x4, waiting for transfers between devices: 69.1 us -> 17.7 us  [the longest x2 14.9 us: to_columns(): lax.all_to_all(value, 'expert', split_axis=1, concat_axis=0, tiled=True)]
    all_to_all x2 -> x0, blocking collectives: 34.3 us -> none  [send(): lax.all_to_all(pack(columns), 'expert', split_axis=0, concat_axis=0, tile...]
    all_gather x0 -> x1, blocking collectives: none -> 13.1 us  [dense_body(): lax.all_gather(jnp.sum(jnp.where(routes[:, :, None] == jnp.arange(local *...]
    all_to_all x2 -> x4, starting transfers between devices: 8.22 us -> 16.9 us  [the longest x2 9.73 us: to_columns(): lax.all_to_all(value, 'expert', split_axis=1, concat_axis=0, tiled=True)]
    gather x3 -> x1, local copies, waits for them, and re-layouts: 7.79 us -> 0.56 us  [dense_body(): share = jnp.repeat(jnp.take(named, experts, axis=1), hidden_width, axis=1)]
  transfers between devices with their start and end apart: 9 -> 6, of which waited for: 8 -> 5; matrix products, arithmetic and copies ran while one was open for 9% -> 7% of each run, Pallas kernels for 0% -> 0%
where the time goes in v1:
time: 272 us; the launch traced here: 271 us
  waiting for transfers between devices  193 us (71%)
  matrix products  19.6 us (7%)
  starting transfers between devices  17 us (6%)
  local copies, waits for them, and re-layouts  14.4 us (5%)
  between operations  14.2 us (5%)
  blocking collectives  13.1 us (5%)
    psum x2, waiting for transfers between devices, total(): return lax.psum(value.astype(bf16), ('expert', 'dp'))  175 us
    dot_general x12, matrix products, dot(): return lax.dot_general(a, b, (dims, ((), ())), preferred_element_type=f32)  19.6 us
    all_to_all x2, waiting for transfers between devices, to_columns(): lax.all_to_all(value, 'expert', split_axis=1, concat_axis=0, tiled=True)  14.9 us
    all_gather x1, blocking collectives, dense_body(): lax.all_gather(jnp.sum(jnp.where(routes[:, :, None] == jnp.arange(local *...  13.1 us
    all_to_all x2, starting transfers between devices, to_columns(): lax.all_to_all(value, 'expert', split_axis=1, concat_axis=0, tiled=True)  9.73 us
    unnamed x42, local copies, waits for them, and re-layouts  8.92 us
    all_to_all x2, starting transfers between devices, to_rows(): lax.all_to_all(value, 'expert', split_axis=0, concat_axis=1, tiled=True)  7.16 us
  transfers between devices with their start and end apart: 6, of which 5 were waited for; matrix products, arithmetic and copies ran while one was open for 7% of the time, Pallas kernels for 0%

profile of v1, /device:TPU:0, one launch (start us, length us, event | category | flops | bytes accessed | tf_op | source)
XLA Modules:
  0.0 271.5 jit_solution(11741762646184264398)
XLA Ops:
  7.2 0.0 copy-start
  7.2 1.9 copy.45
  9.1 6.3 %all-to-all-start = ((bf16[128,4,256]{0,2,1:T(8,128)(2,1)}), bf16[128,4,256]{0,2,1:T(8,128)(2,1)S(1)}, u32[]{:S(2)}, u32[]{:S(2)}) async-start(bf16[128,4,256]{0,2,1:T(8,128)(2,1)} %bitcast.2), calls=%async_computation | async-start | bytes 524288 | tf_op jit(solution)/shard_map/all_to_all | solution.py:116
  15.4 0.8 copy.49
  16.2 8.1 %all-to-all-done = bf16[128,4,256]{0,2,1:T(8,128)(2,1)S(1)} async-done(((bf16[128,4,256]{0,2,1:T(8,128)(2,1)}), bf16[128,4,256]{0,2,1:T(8,128)(2,1)S(1)}, u32[]{:S(2)}, u32[]{:S(2)}) %all-to-all-start) | async-done | bytes 262176 | tf_op jit(solution)/shard_map/all_to_all | solution.py:116
  24.3 3.4 %all-to-all-start.2 = ((bf16[128,4,256]{0,2,1:T(8,128)(2,1)}), bf16[128,4,256]{0,2,1:T(8,128)(2,1)S(1)}, u32[]{:S(2)}, u32[]{:S(2)}) async-start(bf16[128,4,256]{0,2,1:T(8,128)(2,1)} %bitcast.10), calls=%async_computation.2 | async-start | bytes 524288 | tf_op jit(solution)/shard_map/all_to_all | solution.py:116
  27.7 0.0 all-reduce.7.cloned.1.call-start
  27.8 0.1 copy.46
  27.9 6.8 %all-to-all-done.2 = bf16[128,4,256]{0,2,1:T(8,128)(2,1)S(1)} async-done(((bf16[128,4,256]{0,2,1:T(8,128)(2,1)}), bf16[128,4,256]{0,2,1:T(8,128)(2,1)S(1)}, u32[]{:S(2)}, u32[]{:S(2)}) %all-to-all-start.2) | async-done | bytes 262176 | tf_op jit(solution)/shard_map/all_to_all | solution.py:116
  34.7 0.1 copy.50
  34.9 0.0 copy-start.1
  34.9 0.0 copy-start.9
  34.9 1.4 convolution_convert_fusion
  36.3 1.4 convolution_convert_fusion.1
  37.7 0.0 all-reduce.7.cloned.1.call-update
  37.8 0.0 all-reduce.5.cloned.1.call-start
  37.8 0.6 copy-done.16
  38.4 0.0 copy-done.17
  38.4 13.1 %all_gather.3 = f32[512,8]{0,1:T(8,128)S(1)} all-gather(f32[128,8]{0,1:T(8,128)S(1)} %select_reduce_fusion), channel_id=1, replica_groups=mesh['groups'=2,'expert'=4,'dp'=4] {'expert'}, dimensions={0}, use_global_device_ids=true | all-gather | bytes 20480 | tf_op jit(solution)/shard_map/all_gather | solution.py:122
  51.6 0.6 gather_fusion
  52.2 0.1 select_bitcast_fusion
  52.2 0.1 copy.44
  52.4 0.6 broadcast_in_dim.32
  53.0 0.1 copy.57
  53.1 1.5 copy.47
  54.6 80.9 %all-reduce.7.cloned.1.call-done = (bf16[512,1024]{1,0:T(8,128)(2,1)}, bf16[512,1024]{1,0:T(8,128)(2,1)}) async-done(((bf16[512,1024]{1,0:T(8,128)(2,1)}, bf16[512,1024]{1,0:T(8,128)(2,1)}), (bf16[512,1024]{1,0:T(8,128)(2,1)}, bf16[512,1024]{1,0:T(8,128)(2,1)})) %all-reduce.7.cloned.1.call-update) | async-done | bytes 2097168 | tf_op jit(solution)/shard_map/psum | solution.py:113
  135.5 2.1 fusion.2
  137.5 0.8 fusion.1
  138.3 1.7 convolution_convert_fusion.4
  140.1 1.7 convolution_convert_fusion.5
  141.8 0.0 all-reduce.5.cloned.1.call-update
  141.8 1.2 copy-done.6
  143.0 0.1 copy-done.14
  143.1 1.7 convolution_convert_fusion.2
  144.8 94.5 %all-reduce.5.cloned.1.call-done = (bf16[512,1024]{1,0:T(8,128)(2,1)}, bf16[512,1024]{1,0:T(8,128)(2,1)}) async-done(((bf16[512,1024]{1,0:T(8,128)(2,1)}, bf16[512,1024]{1,0:T(8,128)(2,1)}), (bf16[512,1024]{1,0:T(8,128)(2,1)}, bf16[512,1024]{1,0:T(8,128)(2,1)})) %all-reduce.5.cloned.1.call-update) | async-done | bytes 2097168 | tf_op jit(solution)/shard_map/psum | solution.py:113
  239.3 2.5 convolution_convert_fusion.7
  241.8 3.8 %all-to-all-start.1 = ((bf16[4,128,256]{2,1,0:T(8,128)(2,1)}), bf16[4,128,256]{2,1,0:T(8,128)(2,1)S(1)}, u32[]{:S(2)}, u32[]{:S(2)}) async-start(bf16[4,128,256]{2,1,0:T(8,128)(2,1)} %bitcast.75), calls=%async_computation.1 | async-start | bytes 524288 | tf_op jit(solution)/shard_map/all_to_all | solution.py:119
  245.6 1.7 convolution_convert_fusion.3
  247.3 2.4 copy.52
  249.7 1.2 convolution_convert_fusion.6
  250.9 2.8 %all-to-all-done.1 = bf16[4,128,256]{2,1,0:T(8,128)(2,1)S(1)} async-done(((bf16[4,128,256]{2,1,0:T(8,128)(2,1)}), bf16[4,128,256]{2,1,0:T(8,128)(2,1)S(1)}, u32[]{:S(2)}, u32[]{:S(2)}) %all-to-all-start.1) | async-done | bytes 262176 | tf_op jit(solution)/shard_map/all_to_all | solution.py:119
  253.7 3.4 %all-to-all-start.3 = ((bf16[4,128,256]{2,1,0:T(8,128)(2,1)}), bf16[4,128,256]{2,1,0:T(8,128)(2,1)S(1)}, u32[]{:S(2)}, u32[]{:S(2)}) async-start(bf16[4,128,256]{2,1,0:T(8,128)(2,1)} %bitcast.72), calls=%async_computation.3 | async-start | bytes 524288 | tf_op jit(solution)/shard_map/all_to_all | solution.py:119
  257.2 1.7 convolution_bitcast_fusion
  258.9 1.3 copy.54
  260.2 1.7 convolution_bitcast_fusion.1
  261.9 1.3 copy.53
  263.2 0.7 copy.55
  263.9 0.7 copy.56
  (34 shorter events, 0.1 us)
Async XLA Ops:
  7.2 130.4 %copy-start = (bf16[2,256,1024]{2,1,0:T(8,128)(2,1)S(1)}, bf16[2,256,1024]{2,1,0:T(8,128)(2,1)}, u32[]{:S(2)}) copy-start(bf16[2,256,1024]{2,1,0:T(8,128)(2,1)} %param.14) | copy-start | bytes 3145732
  7.2 8.2 %copy-start.15 = (bf16[128,1024]{1,0:T(8,128)(2,1)S(1)}, bf16[128,1024]{1,0:T(8,128)(2,1)}, u32[]{:S(2)}) copy-start(bf16[128,1024]{1,0:T(8,128)(2,1)} %param.15) | copy-start | bytes 786436
  9.1 15.2 %all-to-all-start = ((bf16[128,4,256]{0,2,1:T(8,128)(2,1)}), bf16[128,4,256]{0,2,1:T(8,128)(2,1)S(1)}, u32[]{:S(2)}, u32[]{:S(2)}) async-start(bf16[128,4,256]{0,2,1:T(8,128)(2,1)} %bitcast.2), calls=%async_computation | async-start | bytes 524288 | tf_op jit(solution)/shard_map/all_to_all | solution.py:116
  15.4 19.5 %copy-start.7 = (bf16[256,1024]{1,0:T(8,128)(2,1)S(1)}, bf16[256,1024]{1,0:T(8,128)(2,1)}, u32[]{:S(2)}) copy-start(bf16[256,1024]{1,0:T(8,128)(2,1)} %param.12) | copy-start | bytes 1572868
  24.3 10.4 %all-to-all-start.2 = ((bf16[128,4,256]{0,2,1:T(8,128)(2,1)}), bf16[128,4,256]{0,2,1:T(8,128)(2,1)S(1)}, u32[]{:S(2)}, u32[]{:S(2)}) async-start(bf16[128,4,256]{0,2,1:T(8,128)(2,1)} %bitcast.10), calls=%async_computation.2 | async-start | bytes 524288 | tf_op jit(solution)/shard_map/all_to_all | solution.py:116
  27.7 107.7 %all-reduce.7.cloned.1.call-start = ((), (), s32[]{:S(2)}) async-start(), calls=%async_computation.5 | async-start | bytes 4194304 | tf_op jit(solution)/shard_map/psum | solution.py:113
  34.9 2.9 %copy-start.1 = (bf16[4,128,256]{2,1,0:T(8,128)(2,1)}, bf16[4,128,256]{2,1,0:T(8,128)(2,1)S(1)}, u32[]{:S(2)}) copy-start(bf16[4,128,256]{2,1,0:T(8,128)(2,1)S(1)} %copy.50) | copy-start | bytes 786436
  34.9 1.4 copy-start.9
  37.7 0.7 copy-start.16
  37.7 0.7 copy-start.17
  37.8 201.5 %all-reduce.5.cloned.1.call-start = ((), (), s32[]{:S(2)}) async-start(), calls=%async_computation.4 | async-start | bytes 4194304 | tf_op jit(solution)/shard_map/psum | solution.py:113
  135.5 2.1 copy-start.5
  137.5 2.5 copy-start.13
  138.3 1.7 copy-start.11
  141.8 1.2 copy-start.6
  141.8 1.4 copy-start.14
  143.1 96.2 %copy-start.8 = (bf16[256,1024]{1,0:T(8,128)(2,1)S(1)}, bf16[256,1024]{1,0:T(8,128)(2,1)}, u32[]{:S(2)}) copy-start(bf16[256,1024]{1,0:T(8,128)(2,1)} %param.12) | copy-start | bytes 1572868
  239.3 6.3 %copy-start.4 = (bf16[512,1024]{1,0:T(8,128)(2,1)S(1)}, bf16[512,1024]{1,0:T(8,128)(2,1)}, u32[]{:S(2)}) copy-start(bf16[512,1024]{1,0:T(8,128)(2,1)} %get-tuple-element.32) | copy-start | bytes 3145732
  239.3 6.3 %copy-start.12 = (bf16[512,512]{1,0:T(8,128)(2,1)S(1)}, bf16[512,512]{1,0:T(8,128)(2,1)}, u32[]{:S(2)}) copy-start(bf16[512,512]{1,0:T(8,128)(2,1)} %copy-done.11) | copy-start | bytes 1572868
  241.8 11.9 %all-to-all-start.1 = ((bf16[4,128,256]{2,1,0:T(8,128)(2,1)}), bf16[4,128,256]{2,1,0:T(8,128)(2,1)S(1)}, u32[]{:S(2)}, u32[]{:S(2)}) async-start(bf16[4,128,256]{2,1,0:T(8,128)(2,1)} %bitcast.75), calls=%async_computation.1 | async-start | bytes 524288 | tf_op jit(solution)/shard_map/all_to_all | solution.py:119
  247.3 2.4 copy-start.3
  247.3 2.4 copy-start.10
  249.7 7.4 %copy-start.2 = (bf16[4,128,256]{2,1,0:T(8,128)(2,1)S(1)}, bf16[4,128,256]{2,1,0:T(8,128)(2,1)}, u32[]{:S(2)}) copy-start(bf16[4,128,256]{2,1,0:T(8,128)(2,1)} %copy-done.1) | copy-start | bytes 786436
  253.7 10.2 %all-to-all-start.3 = ((bf16[4,128,256]{2,1,0:T(8,128)(2,1)}), bf16[4,128,256]{2,1,0:T(8,128)(2,1)S(1)}, u32[]{:S(2)}, u32[]{:S(2)}) async-start(bf16[4,128,256]{2,1,0:T(8,128)(2,1)} %bitcast.72), calls=%async_computation.3 | async-start | bytes 524288 | tf_op jit(solution)/shard_map/all_to_all | solution.py:119
Sparse Core Ops, SparseCore 0:
  37.9 97.5 all-reduce.6
  141.9 97.3 all-reduce.4

commit v2 on v0

--- a/solution.py
+++ b/solution.py
@@ -1,6 +1,10 @@
+import functools
+
 import jax
 import jax.numpy as jnp
 from jax import lax
+from jax.experimental import pallas as pl
+from jax.experimental.pallas import tpu as pltpu
 from jax.sharding import PartitionSpec as P
 
 
@@ -100,6 +104,304 @@
     )
 
 
+CHUNKS = 2
+
+
+def fused_kernel(
+    shards,
+    named_ref, tokens_ref, grad_ref, w_in_hbm, w_out_hbm, w_first_hbm, w_second_hbm,
+    mixed_out, grad_tokens_out, grad_w_in_out, grad_w_out_out, grad_first_out, grad_second_out,
+    w_in, w_out, first, second, cols, gates_all, share, twice, hidden, slope,
+    part, from_core, half, from_x, quarter, from_z, whole, back,
+    g_w_in, g_w_out, g_first, g_second,
+    send_sems, recv_sems, local_sems,
+):
+    bf16, f32 = jnp.bfloat16, jnp.float32
+    local, _, width = first.shape
+    rows = from_x.shape[1]
+    block = rows // shards
+    depth = w_in.shape[0]
+    wide, narrow = half.shape[2] * 2, half.shape[2]
+    z, dp = lax.axis_index("expert"), lax.axis_index("dp")
+    core, x = lax.rem(dp, 2), lax.div(dp, 2)
+    core_mate = {"dp": x * 2 + 1 - core}
+    x_mate = {"dp": (1 - x) * 2 + core}
+    peers = [lax.rem(z + d, shards) for d in range(1, shards)]
+    remote, near = [], []
+
+    def at(index, size):
+        return pl.ds(pl.multiple_of(index * size, size), size)
+
+    def ship(src, dst, device):
+        copy = pltpu.make_async_remote_copy(
+            src_ref=src,
+            dst_ref=dst,
+            send_sem=send_sems.at[len(remote)],
+            recv_sem=recv_sems.at[len(remote)],
+            device_id=device,
+            device_id_type=pl.DeviceIdType.MESH,
+        )
+        copy.start()
+        remote.append(copy)
+        return copy
+
+    def move(src, dst):
+        copy = pltpu.make_async_copy(src, dst, local_sems.at[len(near)])
+        copy.start()
+        near.append(copy)
+        return copy
+
+    def dot(a, b, dims):
+        return lax.dot_general(a, b, (dims, ((), ())), preferred_element_type=f32)
+
+    def arrive(copies):
+        for copy in copies:
+            copy.wait_recv()
+
+    barrier = pltpu.get_barrier_semaphore()
+    for device in [core_mate, x_mate] + [{"expert": q} for q in peers]:
+        pl.semaphore_signal(
+            barrier, inc=1, device_id=device, device_id_type=pl.DeviceIdType.MESH
+        )
+    loads = {}
+    loads["w_in"] = move(w_in_hbm, w_in)
+    loads["w_out"] = move(w_out_hbm, w_out)
+    own = {}
+    for h in range(CHUNKS):
+        for a, source in enumerate((tokens_ref, grad_ref)):
+            own[h, a] = move(
+                source.at[pl.ds(h * block, block), at(z, depth)], cols.at[h, a, at(z, block), :]
+            )
+    own_gates = move(named_ref, gates_all.at[z])
+    loads["first"] = move(w_first_hbm, first)
+    loads["second"] = move(w_second_hbm, second)
+    pl.semaphore_wait(barrier, shards + 1)
+
+    incoming = {}
+    for h in range(CHUNKS):
+        for a, source in enumerate((tokens_ref, grad_ref)):
+            incoming[h, a] = [
+                ship(
+                    source.at[pl.ds(h * block, block), at(q, depth)],
+                    cols.at[h, a, at(z, block), :],
+                    {"expert": q},
+                )
+                for q in peers
+            ]
+    gates_in = [ship(named_ref, gates_all.at[z], {"expert": q}) for q in peers]
+
+    def gather_gates():
+        own_gates.wait()
+        arrive(gates_in)
+        total = named_ref.shape[0]
+        expert = lax.broadcasted_iota(jnp.int32, (total, local * width), 0)
+        column = lax.broadcasted_iota(jnp.int32, (total, local * width), 1)
+        pick = jnp.zeros((total, local * width), f32)
+        for j in range(local):
+            hit = (expert == z * local + j) & (column >= j * width) & (column < (j + 1) * width)
+            pick = jnp.where(hit, 1.0, pick)
+        for s in range(shards):
+            value = lax.dot_general(
+                gates_all[s], pick, (((0,), (0,)), ((), ())),
+                precision=lax.Precision.HIGHEST, preferred_element_type=f32,
+            )
+            for h in range(CHUNKS):
+                share[h, s * block : (s + 1) * block, :] = value[h * block : (h + 1) * block]
+
+    def reduce(task, result, h, value):
+        part[task] = value.astype(bf16)
+        mine = core * 2 + x
+        yours = core * 2 + 1 - x
+        copy = ship(part.at[task, :, at(1 - core, narrow)], from_core.at[task], core_mate)
+        yield
+        arrive([copy])
+        half[task, :, at(1 - x, narrow // 2)] = (
+            part[task, :, at(yours, narrow // 2)].astype(f32)
+            + from_core[task, :, at(1 - x, narrow // 2)].astype(f32)
+        ).astype(bf16)
+        copy = ship(half.at[task, :, at(1 - x, narrow // 2)], from_x.at[task], x_mate)
+        yield
+        arrive([copy])
+        quarter[task] = (
+            part[task, :, at(mine, narrow // 2)].astype(f32)
+            + from_core[task, :, at(x, narrow // 2)].astype(f32)
+            + from_x[task].astype(f32)
+        ).astype(bf16)
+        copies = [
+            ship(quarter.at[task, at(q, block), :], from_z.at[task, d], {"expert": q})
+            for d, q in enumerate(peers)
+        ]
+        yield
+        arrive(copies)
+        value = quarter[task, at(z, block), :].astype(f32)
+        for d in range(shards - 1):
+            value = value + from_z[task, d].astype(f32)
+        spot = whole.at[result, pl.ds(pl.multiple_of(h * rows + z * block, block), block), at(mine, narrow // 2)]
+        spot[...] = value.astype(bf16)
+        copies = [ship(spot, spot, {"expert": q}) for q in peers]
+        yield
+        arrive(copies)
+        spot = whole.at[result, pl.ds(h * rows, rows), at(mine, narrow // 2)]
+        copy = ship(spot, spot, x_mate)
+        yield
+        arrive([copy])
+        spot = whole.at[result, pl.ds(h * rows, rows), at(core, narrow)]
+        copy = ship(spot, spot, core_mate)
+        yield
+        arrive([copy])
+
+    def span(h):
+        return slice(h * rows, (h + 1) * rows)
+
+    def give_back(h, a, target):
+        spots = target.at[pl.ds(h * block, block), at(z, depth)]
+        move(back.at[h, a, at(z, block), :], spots)
+        return [ship(back.at[h, a, at(q, block), :], spots, {"expert": q}) for q in peers]
+
+    outgoing = []
+
+    def forward(h):
+        own[h, 0].wait()
+        arrive(incoming[h, 0])
+        if h == 0:
+            loads["w_in"].wait()
+        yield from reduce(h, 0, h, dot(cols[h, 0], w_in[...], ((1,), (0,))))
+        if h == 0:
+            loads["first"].wait()
+            loads["second"].wait()
+            gather_gates()
+        for j in range(local):
+            lanes = slice(j * width, (j + 1) * width)
+            active = jnp.maximum(dot(whole[0, span(h), :], first[j], ((1,), (0,))), 0.0)
+            scaled = share[h, :, lanes] * active
+            hidden[span(h), lanes] = (scaled * active).astype(bf16)
+            twice[h, :, lanes] = 2.0 * scaled
+        yield from reduce(
+            2 * CHUNKS + h, 2, h, dot(hidden[span(h), :], second[...], ((1,), (0,)))
+        )
+        back[h, 0] = dot(whole[2, span(h), :], w_out[...], ((1,), (1,))).astype(bf16)
+        outgoing.extend(give_back(h, 0, mixed_out))
+
+    def backward(h):
+        own[h, 1].wait()
+        arrive(incoming[h, 1])
+        if h == 0:
+            loads["w_out"].wait()
+        yield from reduce(CHUNKS + h, 1, h, dot(cols[h, 1], w_out[...], ((1,), (0,))))
+        slope[span(h), :] = (
+            dot(whole[1, span(h), :], second[...], ((1,), (1,))) * twice[h]
+        ).astype(bf16)
+        value = dot(slope[span(h), 0:width], first[0], ((1,), (1,)))
+        for j in range(1, local):
+            lanes = slice(j * width, (j + 1) * width)
+            value = value + dot(slope[span(h), lanes], first[j], ((1,), (1,)))
+        yield from reduce(3 * CHUNKS + h, 3, h, value)
+        back[h, 1] = dot(whole[3, span(h), :], w_in[...], ((1,), (1,))).astype(bf16)
+        outgoing.extend(give_back(h, 1, grad_tokens_out))
+
+    def weights():
+        for _ in range(7):
+            yield
+        g_second[...] = dot(hidden[...], whole[1], ((0,), (0,))).astype(bf16)
+        move(g_second, grad_second_out)
+        yield
+        for j in range(local):
+            lanes = slice(j * width, (j + 1) * width)
+            g_first[j] = dot(whole[0], slope[:, lanes], ((0,), (0,))).astype(bf16)
+        move(g_first, grad_first_out)
+
+    chains = []
+    for h in range(CHUNKS):
+        chains += [forward(h), backward(h)]
+    chains.append(weights())
+    while chains:
+        for chain in list(chains):
+            try:
+                next(chain)
+            except StopIteration:
+                chains.remove(chain)
+
+    def column(a):
+        return jnp.concatenate([cols[h, a] for h in range(CHUNKS)], axis=0)
+
+    g_w_out[...] = dot(column(1), whole[2], ((0,), (0,)))
+    move(g_w_out, grad_w_out_out)
+    g_w_in[...] = dot(column(0), whole[3], ((0,), (0,)))
+    move(g_w_in, grad_w_in_out)
+    arrive(outgoing)
+    for copy in remote:
+        copy.wait_send()
+    for copy in near[2 * CHUNKS + 5 :]:
+        copy.wait()
+
+
+def fused_layer(tokens, routes, gates, w_in, w_out, w_first, w_second, out_grad):
+    bf16, f32 = jnp.bfloat16, jnp.float32
+    shards = lax.axis_size("expert")
+    local, latent, width = w_first.shape
+    count, depth = tokens.shape[0], w_in.shape[0]
+    rows = count * shards // CHUNKS
+    tasks, ships, moves = 4 * CHUNKS, 4 * CHUNKS * (2 * shards + 2), 8 * CHUNKS + 16
+    ships += (4 * CHUNKS + 1) * (shards - 1)
+    experts = jnp.arange(local * shards, dtype=jnp.int32)[:, None, None]
+    named = jnp.sum(jnp.where(routes.T[None] == experts, gates.T[None], 0.0), axis=1)
+    both = local * width
+    shape = jax.ShapeDtypeStruct
+    outs = pl.pallas_call(
+        functools.partial(fused_kernel, shards),
+        out_shape=[
+            shape(tokens.shape, bf16),
+            shape(tokens.shape, bf16),
+            shape(w_in.shape, f32),
+            shape(w_out.shape, f32),
+            shape(w_first.shape, bf16),
+            shape((both, latent), bf16),
+        ],
+        in_specs=[pl.BlockSpec(memory_space=pltpu.VMEM)] + [pl.BlockSpec(memory_space=pl.ANY)] * 6,
+        out_specs=[pl.BlockSpec(memory_space=pl.ANY)] * 6,
+        scratch_shapes=[
+            pltpu.VMEM(w_in.shape, bf16),
+            pltpu.VMEM(w_out.shape, bf16),
+            pltpu.VMEM(w_first.shape, bf16),
+            pltpu.VMEM((both, latent), bf16),
+            pltpu.VMEM((CHUNKS, 2, rows, depth), bf16),
+            pltpu.VMEM((shards,) + named.shape, f32),
+            pltpu.VMEM((CHUNKS, rows, both), f32),
+            pltpu.VMEM((CHUNKS, rows, both), f32),
+            pltpu.VMEM((CHUNKS * rows, both), bf16),
+            pltpu.VMEM((CHUNKS * rows, both), bf16),
+            pltpu.VMEM((tasks, rows, latent), bf16),
+            pltpu.VMEM((tasks, rows, latent // 2), bf16),
+            pltpu.VMEM((tasks, rows, latent // 2), bf16),
+            pltpu.VMEM((tasks, rows, latent // 4), bf16),
+            pltpu.VMEM((tasks, rows, latent // 4), bf16),
+            pltpu.VMEM((tasks, shards - 1, rows // shards, latent // 4), bf16),
+            pltpu.VMEM((4, CHUNKS * rows, latent), bf16),
+            pltpu.VMEM((CHUNKS, 2, rows, depth), bf16),
+            pltpu.VMEM(w_in.shape, f32),
+            pltpu.VMEM(w_out.shape, f32),
+            pltpu.VMEM(w_first.shape, bf16),
+            pltpu.VMEM((both, latent), bf16),
+            pltpu.SemaphoreType.DMA((ships,)),
+            pltpu.SemaphoreType.DMA((ships,)),
+            pltpu.SemaphoreType.DMA((moves,)),
+        ],
+        compiler_params=pltpu.CompilerParams(
+            collective_id=0, has_side_effects=True, vmem_limit_bytes=56 * 1024 * 1024
+        ),
+        name="fused_layer",
+    )(named, tokens, out_grad, w_in, w_out, w_first, w_second.reshape(both, latent))
+    return (*outs[:5], outs[5].reshape(w_second.shape))
+
+
+def layer(*args):
+    tokens, routes, w_first = args[0], args[1], args[5]
+    count, experts = tokens.shape[0], w_first.shape[0] * lax.axis_size("expert")
+    if 5 * count * routes.shape[1] // (2 * experts) >= count and lax.axis_size("dp") == 4:
+        return fused_layer(*args)
+    return body(*args)
+
+
 def solution(mesh):
     placed = (
         P(("groups", "expert"), "dp"),
@@ -112,7 +414,7 @@
         P(("groups", "expert"), "dp"),
     )
     return jax.shard_map(
-        body,
+        layer,
         mesh=mesh,
         in_specs=placed,
         out_specs=(

time: 427 us -> 118 us (0.28)
  waiting for transfers between devices: 305 us -> 0 us
  Pallas kernels: 0 us -> 106 us
  blocking collectives: 34.3 us -> 0 us
  matrix products: 22.4 us -> 0 us
  local copies, waits for them, and re-layouts: 29.9 us -> 9.89 us
  between operations: 14.4 us -> 0.67 us
  other arithmetic: 11.7 us -> 0.6 us
  starting transfers between devices: 8.68 us -> 0 us
    pallas_call x0 -> x1, Pallas kernels: none -> 106 us  [fused_layer(): pl.pallas_call(functools.partial(fused_kernel, shards), out_shape=[shape(...]
    all_gather x4 -> x0, waiting for transfers between devices: 104 us -> none  [the longest x1 46.4 us: body(): lax.all_gather(w_out, 'expert', axis=0, tiled=True)]
    all_to_all x2 -> x0, waiting for transfers between devices: 69.1 us -> none  [combine_rows(): lax.all_to_all(buffer, 'expert', split_axis=0, concat_axis=0, tiled=True)]
    reduce_scatter x1 -> x0, waiting for transfers between devices: 67.2 us -> none  [body(): lax.psum_scatter(jnp.concatenate([first_term, second_term], axis=1).astyp...]
    psum x2 -> x0, waiting for transfers between devices: 63.2 us -> none  [dp_total(): return lax.psum(value.astype(jnp.bfloat16), 'dp').astype(jnp.float32)]
    all_to_all x2 -> x0, blocking collectives: 34.3 us -> none  [send(): lax.all_to_all(pack(columns), 'expert', split_axis=0, concat_axis=0, tile...]
    dot_general x12 -> x0, matrix products: 22.4 us -> none  [the longest x1 3.09 us: body(): jnp.einsum('sjcl,sjch->jlh', arrived, before_grad, preferred_element_type...]
    all_to_all x2 -> x0, starting transfers between devices: 8.22 us -> none  [combine_rows(): lax.all_to_all(buffer, 'expert', split_axis=0, concat_axis=0, tiled=True)]
  transfers between devices with their start and end apart: 9 -> 0, of which waited for: 8 -> 0; matrix products, arithmetic and copies ran while one was open for 9% -> 0% of each run, Pallas kernels for 0% -> 0%
where the time goes in v2:
time: 118 us; the launch traced here: 117 us
  Pallas kernels  106 us (90%)
  local copies, waits for them, and re-layouts  9.89 us (8%)
    pallas_call x1, Pallas kernels, fused_layer(): pl.pallas_call(functools.partial(fused_kernel, shards), out_shape=[shape(...  106 us
    unnamed x18, local copies, waits for them, and re-layouts  9.89 us

profile of v2, /device:TPU:0, one launch (start us, length us, event | category | flops | bytes accessed | tf_op | source)
XLA Modules:
  0.0 117.3 jit_solution(16674980989426077062)
XLA Ops:
  0.6 0.0 copy-start.5
  0.6 0.0 copy-start.4
  0.7 0.7 copy-done.5
  1.3 0.0 copy-done.4
  1.3 0.6 select_reduce_fusion.named_ref
  1.9 106.1 %fused_layer.1 = (bf16[128,1024]{1,0:T(8,128)(2,1)}, bf16[128,1024]{1,0:T(8,128)(2,1)}, f32[256,1024]{1,0:T(8,128)}, f32[256,1024]{1,0:T(8,128)}, bf16[2,1024,25...) custom-call(f32[8,128]{1,0:T(8,128)} %select_reduce_fusion.named_ref, bf16[128,1024]{1,0:T(8,128)(2,1)} %tokens_ref.1, ...), custom_call_target="tpu_custom_call" | custom-call | tf_op jit(solution)/shard_map/fused_layer/pallas_call | solution.py:350
  108.0 0.0 copy-start.3
  108.1 1.8 %copy.20 = bf16[128,1024]{1,0:T(8,128)(2,1)} copy(bf16[128,1024]{1,0:T(8,128)(2,1)} %get-tuple-element.24) | data formatting | bytes 524288
  109.8 1.7 %copy.21 = bf16[128,1024]{1,0:T(8,128)(2,1)} copy(bf16[128,1024]{1,0:T(8,128)(2,1)} %get-tuple-element.25) | data formatting | bytes 524288
  111.5 0.0 copy-done.3
  111.5 0.0 copy-start.2
  111.5 1.0 copy.22
  112.5 0.6 copy-done.2
  113.1 0.0 copy-start.1
  113.1 1.0 copy.23
  114.1 0.6 copy-done.1
  114.7 0.0 copy-start
  114.7 1.0 copy.24
  115.7 0.6 copy-done
  116.3 1.0 copy.25
Async XLA Ops:
  0.6 0.7 copy-start.5
  0.6 0.7 copy-start.4
  108.0 3.4 %copy-start.3 = (f32[256,1024]{1,0:T(8,128)S(1)}, f32[256,1024]{1,0:T(8,128)}, u32[]{:S(2)}) copy-start(f32[256,1024]{1,0:T(8,128)} %get-tuple-element.26) | copy-start | bytes 3145732
  111.5 1.6 %copy-start.2 = (f32[256,1024]{1,0:T(8,128)S(1)}, f32[256,1024]{1,0:T(8,128)}, u32[]{:S(2)}) copy-start(f32[256,1024]{1,0:T(8,128)} %get-tuple-element.27) | copy-start | bytes 3145732
  113.1 1.6 %copy-start.1 = (bf16[2,1024,256]{2,1,0:T(8,128)(2,1)S(1)}, bf16[2,1024,256]{2,1,0:T(8,128)(2,1)}, u32[]{:S(2)}) copy-start(bf16[2,1024,256]{2,1,0:T(8,128)(2,1)} %get-tuple-element.28) | copy-start | bytes 3145732
  114.7 1.6 %copy-start = (bf16[512,1024]{1,0:T(8,128)(2,1)S(1)}, bf16[512,1024]{1,0:T(8,128)(2,1)}, u32[]{:S(2)}) copy-start(bf16[512,1024]{1,0:T(8,128)(2,1)} %get-tuple-element.17) | copy-start | bytes 3145732

commit v3 on v2

--- a/solution.py
+++ b/solution.py
@@ -105,6 +105,7 @@
 
 
 CHUNKS = 2
+STAGGER = 1
 
 
 def fused_kernel(
@@ -300,8 +301,6 @@
         outgoing.extend(give_back(h, 1, grad_tokens_out))
 
     def weights():
-        for _ in range(7):
-            yield
         g_second[...] = dot(hidden[...], whole[1], ((0,), (0,))).astype(bf16)
         move(g_second, grad_second_out)
         yield
@@ -312,14 +311,18 @@
 
     chains = []
     for h in range(CHUNKS):
-        chains += [forward(h), backward(h)]
-    chains.append(weights())
+        chains += [(STAGGER * len(chains), forward(h))]
+        chains += [(STAGGER * len(chains), backward(h))]
+    chains.append((chains[-1][0] + 7, weights()))
+    turn = 0
     while chains:
-        for chain in list(chains):
-            try:
-                next(chain)
-            except StopIteration:
-                chains.remove(chain)
+        for start, chain in list(chains):
+            if turn >= start:
+                try:
+                    next(chain)
+                except StopIteration:
+                    chains.remove((start, chain))
+        turn += 1
 
     def column(a):
         return jnp.concatenate([cols[h, a] for h in range(CHUNKS)], axis=0)
@@ -333,6 +336,37 @@
         copy.wait_send()
     for copy in near[2 * CHUNKS + 5 :]:
         copy.wait()
+
+
+def settle_kernel(count, *refs):
+    sources, targets, held, sems = refs[:count], refs[count : 2 * count], refs[2 * count : -1], refs[-1]
+    loads = [
+        pltpu.make_async_copy(sources[i], held[i], sems.at[0, i]) for i in range(count)
+    ]
+    stores = [
+        pltpu.make_async_copy(held[i], targets[i], sems.at[1, i]) for i in range(count)
+    ]
+    for copy in loads:
+        copy.start()
+    for load, store in zip(loads, stores):
+        load.wait()
+        store.start()
+    for copy in stores:
+        copy.wait()
+
+
+def settle(*arrays):
+    count = len(arrays)
+    return pl.pallas_call(
+        functools.partial(settle_kernel, count),
+        out_shape=[jax.ShapeDtypeStruct(a.shape, a.dtype) for a in arrays],
+        in_specs=[pl.BlockSpec(memory_space=pl.ANY)] * count,
+        out_specs=[pl.BlockSpec(memory_space=pl.ANY)] * count,
+        scratch_shapes=[pltpu.VMEM(a.shape, a.dtype) for a in arrays]
+        + [pltpu.SemaphoreType.DMA((2, count))],
+        compiler_params=pltpu.CompilerParams(vmem_limit_bytes=56 * 1024 * 1024),
+        name="settle",
+    )(*arrays)
 
 
 def fused_layer(tokens, routes, gates, w_in, w_out, w_first, w_second, out_grad):
@@ -391,6 +425,7 @@
         ),
         name="fused_layer",
     )(named, tokens, out_grad, w_in, w_out, w_first, w_second.reshape(both, latent))
+    outs = settle(*outs)
     return (*outs[:5], outs[5].reshape(w_second.shape))
 
 

time: 118 us -> 98.6 us (0.84)
  Pallas kernels: 106 us -> 96.1 us
  local copies, waits for them, and re-layouts: 9.89 us -> 0.68 us
    pallas_call x1, Pallas kernels: 106 us -> 92 us  [fused_layer(): pl.pallas_call(functools.partial(fused_kernel, shards), out_shape=[shape(...]
    unnamed x18 -> x4, local copies, waits for them, and re-layouts: 9.89 us -> 0.68 us
    pallas_call x0 -> x1, Pallas kernels: none -> 4.1 us  [settle(): pl.pallas_call(functools.partial(settle_kernel, count), out_shape=[jax.Sh...]
where the time goes in v3:
time: 98.6 us; the launch traced here: 98 us
  Pallas kernels  96.1 us (97%)
    pallas_call x1, Pallas kernels, fused_layer(): pl.pallas_call(functools.partial(fused_kernel, shards), out_shape=[shape(...  92 us
    pallas_call x1, Pallas kernels, settle(): pl.pallas_call(functools.partial(settle_kernel, count), out_shape=[jax.Sh...  4.1 us

profile of v3, /device:TPU:0, one launch (start us, length us, event | category | flops | bytes accessed | tf_op | source)
XLA Modules:
  0.0 98.0 jit_solution(10993187848753387791)
XLA Ops:
  0.6 0.0 copy-start.1
  0.6 0.0 copy-start
  0.7 0.7 copy-done.1
  1.3 0.0 copy-done
  1.3 0.6 select_reduce_fusion.named_ref
  1.9 92.0 %fused_layer.1 = (bf16[128,1024]{1,0:T(8,128)(2,1)}, bf16[128,1024]{1,0:T(8,128)(2,1)}, f32[256,1024]{1,0:T(8,128)}, f32[256,1024]{1,0:T(8,128)}, bf16[2,1024,25...) custom-call(f32[8,128]{1,0:T(8,128)} %select_reduce_fusion.named_ref, bf16[128,1024]{1,0:T(8,128)(2,1)} %tokens_ref.1, ...), custom_call_target="tpu_custom_call" | custom-call | tf_op jit(solution)/shard_map/fused_layer/pallas_call | solution.py:384
  93.9 4.1 %settle.1 = (bf16[128,1024]{1,0:T(8,128)(2,1)}, bf16[128,1024]{1,0:T(8,128)(2,1)}, f32[256,1024]{1,0:T(8,128)}, f32[256,1024]{1,0:T(8,128)}, bf16[2,1024,256]{2,1,0:T(8,128)(2,1)}, /*index=5*/bf16[512,1024]{1,0:T(8,128)(2,1)}) custom-call(bf16[128,1024]{1,0:T(8,128)(2,1)} %get-tuple-element.18.refs_0_, bf16[128,1024]{1,0:T(8,128)(2,1)} %get-tuple-element.19.refs_1_, ...), custom_call_target="tpu_custom_call" | custom-call | tf_op jit(solution)/shard_map/settle/pallas_call | solution.py:360
Async XLA Ops:
  0.6 0.7 copy-start.1
  0.6 0.7 copy-start

commit v4 on v3

--- a/solution.py
+++ b/solution.py
@@ -113,21 +113,23 @@
     named_ref, tokens_ref, grad_ref, w_in_hbm, w_out_hbm, w_first_hbm, w_second_hbm,
     mixed_out, grad_tokens_out, grad_w_in_out, grad_w_out_out, grad_first_out, grad_second_out,
     w_in, w_out, first, second, cols, gates_all, share, twice, hidden, slope,
-    part, from_core, half, from_x, quarter, from_z, whole, back,
+    part, from_core, half, from_x, quarter, from_near, pair, from_far, whole, back,
     g_w_in, g_w_out, g_first, g_second,
     send_sems, recv_sems, local_sems,
 ):
     bf16, f32 = jnp.bfloat16, jnp.float32
     local, _, width = first.shape
-    rows = from_x.shape[1]
-    block = rows // shards
+    block = from_far.shape[1]
+    rows = block * shards
     depth = w_in.shape[0]
-    wide, narrow = half.shape[2] * 2, half.shape[2]
+    wide, narrow = part.shape[4], from_core.shape[4]
     z, dp = lax.axis_index("expert"), lax.axis_index("dp")
     core, x = lax.rem(dp, 2), lax.div(dp, 2)
     core_mate = {"dp": x * 2 + 1 - core}
     x_mate = {"dp": (1 - x) * 2 + core}
     peers = [lax.rem(z + d, shards) for d in range(1, shards)]
+    low, high = lax.rem(z, 2), lax.div(z, 2)
+    near_mate, far_mate = {"expert": 2 * high + 1 - low}, {"expert": 2 * (1 - high) + low}
     remote, near = [], []
 
     def at(index, size):
@@ -210,46 +212,73 @@
                 share[h, s * block : (s + 1) * block, :] = value[h * block : (h + 1) * block]
 
     def reduce(task, result, h, value):
-        part[task] = value.astype(bf16)
-        mine = core * 2 + x
-        yours = core * 2 + 1 - x
-        copy = ship(part.at[task, :, at(1 - core, narrow)], from_core.at[task], core_mate)
+        mine, yours = core * 2 + x, core * 2 + 1 - x
+        fine = narrow // 2
+
+        def rows_of(index):
+            start = pl.multiple_of(h * rows + index * block, block)
+            return whole.at[result, pl.ds(start, block), at(mine, fine)]
+
+        def spread(index):
+            spot = rows_of(index)
+            x_copies.append(ship(spot, spot, x_mate))
+            core_copies.append(ship(spot, spot, core_mate))
+
+        x_copies, core_copies = [], []
+        part[task] = value.astype(bf16).reshape(2, 2, block, wide)
+        copy = ship(part.at[task, :, :, :, at(1 - core, narrow)], from_core.at[task], core_mate)
         yield
         arrive([copy])
-        half[task, :, at(1 - x, narrow // 2)] = (
-            part[task, :, at(yours, narrow // 2)].astype(f32)
-            + from_core[task, :, at(1 - x, narrow // 2)].astype(f32)
+        half[task] = (
+            part[task, :, :, :, at(yours, fine)].astype(f32)
+            + from_core[task, :, :, :, at(1 - x, fine)].astype(f32)
         ).astype(bf16)
-        copy = ship(half.at[task, :, at(1 - x, narrow // 2)], from_x.at[task], x_mate)
+        first_copy, second_copy = [
+            ship(half.at[task, :, side], from_x.at[task, :, side], x_mate)
+            for side in (1 - low, low)
+        ]
+        yield
+        arrive([first_copy])
+        quarter[task] = (
+            part[task, :, 1 - low, :, at(mine, fine)].astype(f32)
+            + from_core[task, :, 1 - low, :, at(x, fine)].astype(f32)
+            + from_x[task, :, 1 - low].astype(f32)
+        ).astype(bf16)
+        copy = ship(quarter.at[task], from_near.at[task], near_mate)
+        yield
+        arrive([second_copy, copy])
+
+        def summed(side):
+            return (
+                part[task, side, low, :, at(mine, fine)].astype(f32)
+                + from_core[task, side, low, :, at(x, fine)].astype(f32)
+                + from_x[task, side, low].astype(f32)
+                + from_near[task, side].astype(f32)
+            )
+
+        pair[task] = summed(1 - high).astype(bf16)
+        copy = ship(pair.at[task], from_far.at[task], far_mate)
         yield
         arrive([copy])
-        quarter[task] = (
-            part[task, :, at(mine, narrow // 2)].astype(f32)
-            + from_core[task, :, at(x, narrow // 2)].astype(f32)
-            + from_x[task].astype(f32)
-        ).astype(bf16)
-        copies = [
-            ship(quarter.at[task, at(q, block), :], from_z.at[task, d], {"expert": q})
-            for d, q in enumerate(peers)
-        ]
-        yield
-        arrive(copies)
-        value = quarter[task, at(z, block), :].astype(f32)
-        for d in range(shards - 1):
-            value = value + from_z[task, d].astype(f32)
-        spot = whole.at[result, pl.ds(pl.multiple_of(h * rows + z * block, block), block), at(mine, narrow // 2)]
-        spot[...] = value.astype(bf16)
-        copies = [ship(spot, spot, {"expert": q}) for q in peers]
-        yield
-        arrive(copies)
-        spot = whole.at[result, pl.ds(h * rows, rows), at(mine, narrow // 2)]
-        copy = ship(spot, spot, x_mate)
-        yield
-        arrive([copy])
-        spot = whole.at[result, pl.ds(h * rows, rows), at(core, narrow)]
+        rows_of(z)[...] = (summed(high) + from_far[task].astype(f32)).astype(bf16)
+        far_copy = ship(rows_of(z), rows_of(z), far_mate)
+        near_copy = ship(rows_of(z), rows_of(z), near_mate)
+        spread(z)
+        yield
+        arrive([far_copy])
+        other = low + 2 * (1 - high)
+        copy = ship(rows_of(other), rows_of(other), near_mate)
+        spread(other)
+        yield
+        arrive([near_copy, copy])
+        spread(1 - low)
+        spread(3 - low)
+        yield
+        arrive(x_copies)
+        spot = whole.at[result, pl.ds(h * rows, rows), at(yours, fine)]
         copy = ship(spot, spot, core_mate)
         yield
-        arrive([copy])
+        arrive(core_copies + [copy])
 
     def span(h):
         return slice(h * rows, (h + 1) * rows)
@@ -313,7 +342,7 @@
     for h in range(CHUNKS):
         chains += [(STAGGER * len(chains), forward(h))]
         chains += [(STAGGER * len(chains), backward(h))]
-    chains.append((chains[-1][0] + 7, weights()))
+    chains.append((chains[-1][0] + 9, weights()))
     turn = 0
     while chains:
         for start, chain in list(chains):
@@ -374,8 +403,8 @@
     shards = lax.axis_size("expert")
     local, latent, width = w_first.shape
     count, depth = tokens.shape[0], w_in.shape[0]
-    rows = count * shards // CHUNKS
-    tasks, ships, moves = 4 * CHUNKS, 4 * CHUNKS * (2 * shards + 2), 8 * CHUNKS + 16
+    rows, block = count * shards // CHUNKS, count // CHUNKS
+    tasks, ships, moves = 4 * CHUNKS, 4 * CHUNKS * 18, 8 * CHUNKS + 16
     ships += (4 * CHUNKS + 1) * (shards - 1)
     experts = jnp.arange(local * shards, dtype=jnp.int32)[:, None, None]
     named = jnp.sum(jnp.where(routes.T[None] == experts, gates.T[None], 0.0), axis=1)
@@ -404,12 +433,14 @@
             pltpu.VMEM((CHUNKS, rows, both), f32),
             pltpu.VMEM((CHUNKS * rows, both), bf16),
             pltpu.VMEM((CHUNKS * rows, both), bf16),
-            pltpu.VMEM((tasks, rows, latent), bf16),
-            pltpu.VMEM((tasks, rows, latent // 2), bf16),
-            pltpu.VMEM((tasks, rows, latent // 2), bf16),
-            pltpu.VMEM((tasks, rows, latent // 4), bf16),
-            pltpu.VMEM((tasks, rows, latent // 4), bf16),
-            pltpu.VMEM((tasks, shards - 1, rows // shards, latent // 4), bf16),
+            pltpu.VMEM((tasks, 2, 2, block, latent), bf16),
+            pltpu.VMEM((tasks, 2, 2, block, latent // 2), bf16),
+            pltpu.VMEM((tasks, 2, 2, block, latent // 4), bf16),
+            pltpu.VMEM((tasks, 2, 2, block, latent // 4), bf16),
+            pltpu.VMEM((tasks, 2, block, latent // 4), bf16),
+            pltpu.VMEM((tasks, 2, block, latent // 4), bf16),
+            pltpu.VMEM((tasks, block, latent // 4), bf16),
+            pltpu.VMEM((tasks, block, latent // 4), bf16),
             pltpu.VMEM((4, CHUNKS * rows, latent), bf16),
             pltpu.VMEM((CHUNKS, 2, rows, depth), bf16),
             pltpu.VMEM(w_in.shape, f32),
@@ -431,8 +462,9 @@
 
 def layer(*args):
     tokens, routes, w_first = args[0], args[1], args[5]
-    count, experts = tokens.shape[0], w_first.shape[0] * lax.axis_size("expert")
-    if 5 * count * routes.shape[1] // (2 * experts) >= count and lax.axis_size("dp") == 4:
+    shards = lax.axis_size("expert")
+    count, experts = tokens.shape[0], w_first.shape[0] * shards
+    if 5 * count * routes.shape[1] // (2 * experts) >= count and lax.axis_size("dp") == 4 == shards:
         return fused_layer(*args)
     return body(*args)
 

time: 98.6 us -> 92.6 us (0.939)
  Pallas kernels: 96.1 us -> 90.1 us
    pallas_call x1, Pallas kernels: 92 us -> 86 us  [fused_layer(): pl.pallas_call(functools.partial(fused_kernel, shards), out_shape=[shape(...]
where the time goes in v4:
time: 92.6 us; the launch traced here: 92.1 us
  Pallas kernels  90.1 us (97%)
    pallas_call x1, Pallas kernels, fused_layer(): pl.pallas_call(functools.partial(fused_kernel, shards), out_shape=[shape(...  86 us
    pallas_call x1, Pallas kernels, settle(): pl.pallas_call(functools.partial(settle_kernel, count), out_shape=[jax.Sh...  4.1 us

profile of v4, /device:TPU:0, one launch (start us, length us, event | category | flops | bytes accessed | tf_op | source)
XLA Modules:
  0.0 92.1 jit_solution(12113954264779446156)
XLA Ops:
  0.6 0.0 copy-start.1
  0.6 0.0 copy-start
  0.7 0.7 copy-done.1
  1.3 0.0 copy-done
  1.3 0.6 select_reduce_fusion.named_ref
  1.9 86.0 %fused_layer.1 = (bf16[128,1024]{1,0:T(8,128)(2,1)}, bf16[128,1024]{1,0:T(8,128)(2,1)}, f32[256,1024]{1,0:T(8,128)}, f32[256,1024]{1,0:T(8,128)}, bf16[2,1024,25...) custom-call(f32[8,128]{1,0:T(8,128)} %select_reduce_fusion.named_ref, bf16[128,1024]{1,0:T(8,128)(2,1)} %tokens_ref.1, ...), custom_call_target="tpu_custom_call" | custom-call | tf_op jit(solution)/shard_map/fused_layer/pallas_call | solution.py:413
  88.0 4.1 %settle.1 = (bf16[128,1024]{1,0:T(8,128)(2,1)}, bf16[128,1024]{1,0:T(8,128)(2,1)}, f32[256,1024]{1,0:T(8,128)}, f32[256,1024]{1,0:T(8,128)}, bf16[2,1024,256]{2,1,0:T(8,128)(2,1)}, /*index=5*/bf16[512,1024]{1,0:T(8,128)(2,1)}) custom-call(bf16[128,1024]{1,0:T(8,128)(2,1)} %get-tuple-element.18.refs_0_, bf16[128,1024]{1,0:T(8,128)(2,1)} %get-tuple-element.19.refs_1_, ...), custom_call_target="tpu_custom_call" | custom-call | tf_op jit(solution)/shard_map/settle/pallas_call | solution.py:389
Async XLA Ops:
  0.6 0.7 copy-start.1
  0.6 0.7 copy-start
